TPU v7x, 32 devices: a whole 2x2x4 slice. The times are simulated.
32 devices in a mesh: dp: 16 (over z, x, core), blk: 2 (over y).
Axes of the slice: x: 2, y: 2, z: 4, core: 2. Of those that a mesh axis runs over, the one named last changes fastest.
Arguments:
- waveform: bfloat16 [512, 330], P(('dp', 'blk')), may hold values from -6 to 6
- length_bin: int32 [512], P(('dp', 'blk')), may hold values from 1 to 4
- packing: int32 [32, 16], P(('dp', 'blk')), may hold values from 0 to 15, each once within a row
- cotangent: bfloat16 [512, 32, 512], P(('dp', 'blk')), may hold values from -6 to 6
- conv_one: bfloat16 [10, 512], replicated, may hold values from -2 to 2
- bias_one: float32 [512], replicated, may hold values from -6 to 6
- gain_one: float32 [512], replicated, may hold values from 2 to 8
- shift_one: float32 [512], replicated, may hold values from -12 to 12
- conv_two: bfloat16 [1536, 512], replicated, may hold values from -0.15625 to 0.15625
- bias_two: float32 [512], replicated, may hold values from -6 to 6
- gain_two: float32 [512], replicated, may hold values from 0.5 to 1.5
- shift_two: float32 [512], replicated, may hold values from -3 to 3
Outputs:
- grad_conv_two: float32 [1536, 512], P('dp')
- grad_small: float32 [16, 512], replicated
All inputs are finite; a program needn't handle non-finite values.
Results may differ from a plain program's by a relative error of at most 0.0046.
Values may be sent and summed in bfloat16 or wider, within the bound.
No kernel may reach another device: no remote copies, remote signals or barrier semaphores. Data moves between devices by JAX's collectives and lax.ppermute only.
A program may use at most 64 MiB of HBM per device.

v0:
```python
import jax
import jax.numpy as jnp
from jax import lax
from jax.sharding import PartitionSpec as P

NB = 4
GROUP = 8


def norm_act(z, gain, shift):
    mean = jnp.mean(z, axis=-1, keepdims=True)
    cent = z - mean
    var = jnp.mean(cent * cent, axis=-1, keepdims=True)
    rstd = lax.rsqrt(var + 1e-05)
    normed = cent * rstd
    return (normed * gain + shift, normed, rstd)


def gelu_exact(act):
    return 0.5 * act * (1.0 + lax.erf(act * 0.7071067811865476))


def norm_back(grad_out, act, normed, rstd, gain):
    cdf = 0.5 * (1.0 + lax.erf(act * 0.7071067811865476))
    pdf = jnp.exp(-0.5 * act * act) * 0.3989422804014327
    grad_act = grad_out * (cdf + act * pdf)
    grad_gain = jnp.sum(grad_act * normed, axis=0)
    grad_shift = jnp.sum(grad_act, axis=0)
    grad_norm = grad_act * gain
    inner = grad_norm - jnp.mean(grad_norm, axis=-1, keepdims=True)
    inner = inner - normed * jnp.mean(grad_norm * normed, axis=-1, keepdims=True)
    return (rstd * inner, grad_gain, grad_shift)


def pass_group(
    wave,
    bins,
    cot,
    conv_one,
    bias_one,
    gain_one,
    shift_one,
    conv_two,
    bias_two,
    gain_two,
    shift_two,
):
    count = wave.shape[0]
    frames_two = cot.shape[1]
    width = cot.shape[2]
    frames_one = 2 * frames_two + 1
    split = wave.reshape(count, frames_one + 1, 5)
    cols_one = jnp.concatenate([split[:, :-1], split[:, 1:]], axis=-1).reshape(
        count * frames_one, 10
    )
    z_one = jnp.dot(cols_one, conv_one, preferred_element_type=jnp.float32) + bias_one
    act_one, normed_one, rstd_one = norm_act(z_one, gain_one, shift_one)
    hidden = gelu_exact(act_one).astype(jnp.bfloat16).reshape(count, frames_one, width)
    cols_two = jnp.concatenate(
        [hidden[:, : 2 * frames_two].reshape(count, frames_two, 2 * width), hidden[:, 2::2]],
        axis=-1,
    )
    cols_two = cols_two.reshape(count * frames_two, 3 * width)
    z_two = jnp.dot(cols_two, conv_two, preferred_element_type=jnp.float32) + bias_two
    act_two, normed_two, rstd_two = norm_act(z_two, gain_two, shift_two)
    limit = bins * frames_two // NB
    valid = (jnp.arange(frames_two, dtype=jnp.int32)[None, :] < limit[:, None]).astype(jnp.float32)
    grad_out = (cot.astype(jnp.float32) * valid[:, :, None]).reshape(count * frames_two, width)
    dz_two, dgain_two, dshift_two = norm_back(grad_out, act_two, normed_two, rstd_two, gain_two)
    dbias_two = jnp.sum(dz_two, axis=0)
    dz_two_b = dz_two.astype(jnp.bfloat16)
    dcols = jnp.dot(dz_two_b, conv_two.T, preferred_element_type=jnp.float32).reshape(
        count, frames_two, 3 * width
    )
    part_a = dcols[:, :, : 2 * width].reshape(count, 2 * frames_two, width)
    part_b = dcols[:, :, 2 * width :]
    spread = jnp.stack([part_b, jnp.zeros_like(part_b)], axis=2).reshape(
        count, 2 * frames_two, width
    )
    zero_one = jnp.zeros((count, 1, width), jnp.float32)
    zero_two = jnp.zeros((count, 2, width), jnp.float32)
    dhidden = jnp.concatenate([part_a, zero_one], axis=1) + jnp.concatenate(
        [zero_two, spread[:, : 2 * frames_two - 1]], axis=1
    )
    dz_one, dgain_one, dshift_one = norm_back(
        dhidden.reshape(count * frames_one, width), act_one, normed_one, rstd_one, gain_one
    )
    dbias_one = jnp.sum(dz_one, axis=0)
    dconv_one = jnp.dot(cols_one.T, dz_one.astype(jnp.bfloat16), preferred_element_type=jnp.float32)
    small = jnp.concatenate(
        [
            dconv_one,
            jnp.stack([dbias_one, dgain_one, dshift_one, dbias_two, dgain_two, dshift_two]),
        ],
        axis=0,
    )
    return (cols_two, dz_two_b, small)


def per_device(
    waveform,
    length_bin,
    packing,
    cotangent,
    conv_one,
    bias_one,
    gain_one,
    shift_one,
    conv_two,
    bias_two,
    gain_two,
    shift_two,
):
    order_list = packing[0]
    sent_wave = waveform[order_list]
    sent_bins = length_bin[order_list]
    wave, bins = (
        lax.all_to_all(sent_wave, "dp", split_axis=0, concat_axis=0, tiled=True),
        lax.all_to_all(sent_bins, "dp", split_axis=0, concat_axis=0, tiled=True),
    )
    count = wave.shape[0]
    record = wave.shape[1]
    frames_two = cotangent.shape[1]
    width = cotangent.shape[2]
    groups = count // GROUP
    xs = (
        wave.reshape(groups, GROUP, record),
        bins.reshape(groups, GROUP),
        cotangent.reshape(groups, GROUP, frames_two, width),
    )

    def step(small_sum, item):
        cols_two, dz_two_b, small = pass_group(
            item[0],
            item[1],
            item[2],
            conv_one,
            bias_one,
            gain_one,
            shift_one,
            conv_two,
            bias_two,
            gain_two,
            shift_two,
        )
        return (small_sum + small, (cols_two, dz_two_b))

    small_local, stacked = lax.scan(step, jnp.zeros((16, width), jnp.float32), xs)
    cols_all = stacked[0].reshape(count * frames_two, 3 * width)
    dz_all = stacked[1].reshape(count * frames_two, width)
    term = lax.dot_general(
        cols_all, dz_all, (((0,), (0,)), ((), ())), preferred_element_type=jnp.float32
    )
    whole = lax.psum(term, "blk")
    share = lax.psum_scatter(whole, "dp", scatter_dimension=0, tiled=True)
    small_total = lax.psum(small_local, ("dp", "blk"))
    return (share, small_total)


def solution(mesh):
    return jax.shard_map(
        per_device,
        mesh=mesh,
        in_specs=(
            P(("dp", "blk"), None),
            P(("dp", "blk")),
            P(("dp", "blk"), None),
            P(("dp", "blk"), None, None),
            P(),
            P(),
            P(),
            P(),
            P(),
            P(),
            P(),
            P(),
        ),
        out_specs=(P("dp", None), P()),
        check_vma=False,
    )
```

profile of v0, /device:TPU:0, one launch (start us, length us, event | category | flops | bytes accessed | tf_op | source)
XLA Modules:
  0.0 192.3 jit_solution(11816954975854196462)
XLA Ops:
  7.2 0.7 fusion.21
  7.9 1.3 gather_fusion.1
  9.2 0.7 copy.29
  9.9 7.4 %all-to-all-start.1 = ((s32[16,1,1]{2,1,0:T(1,128)}), s32[16,1,1]{2,1,0:T(1,128)S(1)}, u32[]{:S(2)}, u32[]{:S(2)}) async-start(s32[16,1,1]{2,1,0:T(1,128)} %copy.29), calls=%async_computation.1 | async-start | bytes 16384 | tf_op jit(solution)/shard_map/all_to_all | solution.py:119
  17.2 0.6 gather_fusion
  17.8 0.5 broadcast.360
  18.3 0.7 reduce.1
  19.0 0.7 reshape.260
  19.7 3.9 %all-to-all-done.1 = s32[16,1,1]{2,1,0:T(1,128)S(1)} async-done(((s32[16,1,1]{2,1,0:T(1,128)}), s32[16,1,1]{2,1,0:T(1,128)S(1)}, u32[]{:S(2)}, u32[]{:S(2)}) %all-to-all-start.1) | async-done | bytes 96 | tf_op jit(solution)/shard_map/all_to_all | solution.py:119
  23.6 3.5 %all-to-all-start = ((bf16[16,2,165]{2,1,0:T(2,128)(2,1)}), bf16[16,2,165]{2,1,0:T(2,128)(2,1)S(1)}, u32[]{:S(2)}, u32[]{:S(2)}) async-start(bf16[16,2,165]{2,1,0:T(2,128)(2,1)} %reshape.260), calls=%async_computation | async-start | bytes 32768 | tf_op jit(solution)/shard_map/all_to_all | solution.py:118
  27.5 0.7 reshape.230
  28.2 5.3 %all-to-all-done = bf16[16,2,165]{2,1,0:T(2,128)(2,1)S(1)} async-done(((bf16[16,2,165]{2,1,0:T(2,128)(2,1)}), bf16[16,2,165]{2,1,0:T(2,128)(2,1)S(1)}, u32[]{:S(2)}, u32[]{:S(2)}) %all-to-all-start) | async-done | bytes 10592 | tf_op jit(solution)/shard_map/all_to_all | solution.py:118
  33.6 0.6 copy.35
  34.2 41.1 %while.17 = (s32[]{:T(128)}, f32[16,512]{1,0:T(8,128)}, bf16[2,256,1536]{2,1,0:T(8,128)(2,1)}, bf16[2,256,512]{2,1,0:T(8,128)(2,1)}, bf16[2,8,330]{2,1,0:T(8,128...) while((s32[]{:T(128)}, f32[16,512]{1,0:T(8,128)}, ...), condition=%wide.region_15.16_spmd.clone, body=%wide.region_0.15_spmd.clone.sunk | while | flops 835685888 | bytes 56027588 | solution.py:148
  34.2 0.7 and_select_fusion.2
  35.1 0.7 constant_dynamic-slice_fusion.5
  36.6 0.4 fusion.58
  39.0 2.1 %fusion.59 = (f32[256]{0:T(256)S(1)}, f32[256,512]{1,0:T(8,128)S(1)}) fusion(f32[512]{0:T(512)S(1)} %copy-done.11, bf16[1536,512]{1,0:T(8,128)(2,1)} %get-tuple-element.475, bf16[256,512]{1,0:T(8,128)(2,1)S(1)} %bitcast.85, bf16[256,1024]{1,0:T(8,128)(2,1)S(1)} %concatenate.58), kind=kOutput, calls=%fused_computation.73.clone.1 | convolution fusion | flops 404487936 | bytes 2886656 | tf_op jit(solution)/shard_map/while/body/eval_jaxpr/dot_general | solution.py:64
  41.4 0.6 multiply_reduce_fusion.14
  42.4 0.8 copy-done.10
  43.3 0.9 maximum_dynamic-update-slice_fusion.2
  44.2 0.8 copy-done.1
  45.0 0.6 fusion.61
  45.6 0.8 slice_bitcast_fusion.2
  46.7 1.6 copy.42
  48.6 1.7 reshape.273
  50.4 1.5 pad_add_fusion.2
  52.0 1.1 multiply_reduce_fusion.15
  53.8 0.6 select_add_fusion.2
  54.4 0.7 and_select_fusion.2
  55.3 0.7 constant_dynamic-slice_fusion.5
  56.8 0.4 fusion.58
  59.2 2.1 %fusion.59 = (f32[256]{0:T(256)S(1)}, f32[256,512]{1,0:T(8,128)S(1)}) fusion(f32[512]{0:T(512)S(1)} %copy-done.11, bf16[1536,512]{1,0:T(8,128)(2,1)} %get-tuple-element.475, bf16[256,512]{1,0:T(8,128)(2,1)S(1)} %bitcast.85, bf16[256,1024]{1,0:T(8,128)(2,1)S(1)} %concatenate.58), kind=kOutput, calls=%fused_computation.73.clone.1 | convolution fusion | flops 404487936 | bytes 2886656 | tf_op jit(solution)/shard_map/while/body/eval_jaxpr/dot_general | solution.py:64
  61.6 0.6 multiply_reduce_fusion.14
  62.6 0.8 copy-done.10
  63.5 0.9 maximum_dynamic-update-slice_fusion.2
  64.4 0.8 copy-done.1
  65.2 0.6 fusion.61
  65.8 0.8 slice_bitcast_fusion.2
  66.9 1.6 copy.42
  68.8 1.7 reshape.273
  70.6 1.5 pad_add_fusion.2
  72.2 1.1 multiply_reduce_fusion.15
  74.0 1.4 select_add_fusion.2
  75.4 4.2 %convolution_bitcast_fusion = f32[1536,512]{1,0:T(8,128)} fusion(bf16[2,256,1536]{2,1,0:T(8,128)(2,1)} %get-tuple-element.190, bf16[2,256,512]{2,1,0:T(8,128)(2,1)} %get-tuple-element.191), kind=kOutput, calls=%fused_computation.65 | convolution fusion | flops 805306368 | bytes 5242880 | tf_op jit(solution)/shard_map/dot_general | solution.py:151
  79.6 63.6 %reduce-scatter.2.cloned.1.call-done = f32[96,512]{1,0:T(8,128)} async-done(((f32[1536,512]{1,0:T(8,128)}), f32[96,512]{1,0:T(8,128)}) %reduce-scatter.2.cloned.1.call-update) | async-done | bytes 196624 | tf_op jit(solution)/shard_map/reduce_scatter | solution.py:155
  143.3 40.6 %psum.15 = f32[16,512]{1,0:T(8,128)} all-reduce(f32[16,512]{1,0:T(8,128)} %get-tuple-element.192), channel_id=1, replica_groups=mesh['dp'=16,'blk'=2] {'dp','blk'}, use_global_device_ids=true, to_apply=%region_18.19 | all-reduce | flops 8192 | bytes 65536 | tf_op jit(solution)/shard_map/psum | solution.py:156
  183.9 1.6 copy.58
  (119 shorter events, 10.3 us)
Async XLA Ops:
  7.2 10.1 %copy-start = (bf16[16,330]{1,0:T(8,128)(2,1)S(1)}, bf16[16,330]{1,0:T(8,128)(2,1)}, u32[]{:S(2)}) copy-start(bf16[16,330]{1,0:T(8,128)(2,1)} %param.14) | copy-start | bytes 31684
  9.9 13.7 %all-to-all-start.1 = ((s32[16,1,1]{2,1,0:T(1,128)}), s32[16,1,1]{2,1,0:T(1,128)S(1)}, u32[]{:S(2)}, u32[]{:S(2)}) async-start(s32[16,1,1]{2,1,0:T(1,128)} %copy.29), calls=%async_computation.1 | async-start | bytes 16384 | tf_op jit(solution)/shard_map/all_to_all | solution.py:119
  23.6 10.0 %all-to-all-start = ((bf16[16,2,165]{2,1,0:T(2,128)(2,1)}), bf16[16,2,165]{2,1,0:T(2,128)(2,1)S(1)}, u32[]{:S(2)}, u32[]{:S(2)}) async-start(bf16[16,2,165]{2,1,0:T(2,128)(2,1)} %reshape.260), calls=%async_computation | async-start | bytes 32768 | tf_op jit(solution)/shard_map/all_to_all | solution.py:118
  27.1 116.2 %reduce-scatter.2.cloned.1.call-start = ((), (), s32[]{:S(2)}) async-start(), calls=%async_computation.3 | async-start | bytes 3342336 | tf_op jit(solution)/shard_map/reduce_scatter | solution.py:155
  34.2 2.3 %copy-start.2 = (bf16[2,8,32,512]{3,2,1,0:T(8,128)(2,1)S(1)}, bf16[2,8,32,512]{3,2,1,0:T(8,128)(2,1)}, u32[]{:S(2)}) copy-start(bf16[2,8,32,512]{3,2,1,0:T(8,128)(2,1)} %get-tuple-element.477) | copy-start | bytes 1572868 | tf_op jit(solution)/shard_map/while
  34.2 2.3 %copy-start.4 = (bf16[10,512]{1,0:T(8,128)(2,1)S(1)}, bf16[10,512]{1,0:T(8,128)(2,1)}, u32[]{:S(2)}) copy-start(bf16[10,512]{1,0:T(8,128)(2,1)} %get-tuple-element.471) | copy-start | bytes 30724 | tf_op jit(solution)/shard_map/while
  34.2 2.3 %copy-start.7 = (f32[512]{0:T(512)S(1)}, f32[512]{0:T(512)}, u32[]{:S(2)}) copy-start(f32[512]{0:T(512)} %get-tuple-element.472) | copy-start | bytes 6148 | tf_op jit(solution)/shard_map/while
  36.5 0.8 copy-start.3
  36.5 0.8 copy-start.5
  38.4 0.7 copy-start.11
  39.0 2.3 %copy-start.6 = (f32[512]{0:T(512)S(1)}, f32[512]{0:T(512)}, u32[]{:S(2)}) copy-start(f32[512]{0:T(512)} %get-tuple-element.479) | copy-start | bytes 6148 | tf_op jit(solution)/shard_map/while
  39.0 2.3 %copy-start.8 = (f32[512]{0:T(512)S(1)}, f32[512]{0:T(512)}, u32[]{:S(2)}) copy-start(f32[512]{0:T(512)} %get-tuple-element.480) | copy-start | bytes 6148 | tf_op jit(solution)/shard_map/while
  41.1 1.0 copy-start.9
  42.4 0.8 copy-start.10
  43.3 1.7 copy-start.1
  54.4 2.3 %copy-start.2 = (bf16[2,8,32,512]{3,2,1,0:T(8,128)(2,1)S(1)}, bf16[2,8,32,512]{3,2,1,0:T(8,128)(2,1)}, u32[]{:S(2)}) copy-start(bf16[2,8,32,512]{3,2,1,0:T(8,128)(2,1)} %get-tuple-element.477) | copy-start | bytes 1572868 | tf_op jit(solution)/shard_map/while
  54.4 2.3 %copy-start.4 = (bf16[10,512]{1,0:T(8,128)(2,1)S(1)}, bf16[10,512]{1,0:T(8,128)(2,1)}, u32[]{:S(2)}) copy-start(bf16[10,512]{1,0:T(8,128)(2,1)} %get-tuple-element.471) | copy-start | bytes 30724 | tf_op jit(solution)/shard_map/while
  54.4 2.3 %copy-start.7 = (f32[512]{0:T(512)S(1)}, f32[512]{0:T(512)}, u32[]{:S(2)}) copy-start(f32[512]{0:T(512)} %get-tuple-element.472) | copy-start | bytes 6148 | tf_op jit(solution)/shard_map/while
  56.7 0.8 copy-start.3
  56.7 0.8 copy-start.5
  58.6 0.7 copy-start.11
  59.2 2.3 %copy-start.6 = (f32[512]{0:T(512)S(1)}, f32[512]{0:T(512)}, u32[]{:S(2)}) copy-start(f32[512]{0:T(512)} %get-tuple-element.479) | copy-start | bytes 6148 | tf_op jit(solution)/shard_map/while
  59.2 2.3 %copy-start.8 = (f32[512]{0:T(512)S(1)}, f32[512]{0:T(512)}, u32[]{:S(2)}) copy-start(f32[512]{0:T(512)} %get-tuple-element.480) | copy-start | bytes 6148 | tf_op jit(solution)/shard_map/while
  61.3 1.0 copy-start.9
  62.6 0.8 copy-start.10
  63.5 1.7 copy-start.1
  79.6 104.3 %all-reduce.5.cloned.1.call-start = ((), (), s32[]{:S(2)}) async-start(), calls=%async_computation.4 | async-start | bytes 393216 | tf_op jit(solution)/shard_map/psum | solution.py:154
Sparse Core Ops, SparseCore 0:
  79.7 63.4 reduce-scatter.1
  145.5 21.4 all-reduce.4
where the time goes:
time: 193 us; the launch traced here: 192 us
  waiting for transfers between devices  72.8 us (38%)
  blocking collectives  40.6 us (21%)
  local copies, waits for them, and re-layouts  25.6 us (13%)
  other arithmetic  16.9 us (9%)
  between operations  14.1 us (7%)
  starting transfers between devices  10.9 us (6%)
  matrix products  10.8 us (6%)
    reduce_scatter x1, waiting for transfers between devices, per_device(): share = lax.psum_scatter(whole, 'dp', scatter_dimension=0, tiled=True)  63.6 us
    psum x1, blocking collectives, per_device(): small_total = lax.psum(small_local, ('dp', 'blk'))  40.6 us
    all_to_all x1, starting transfers between devices, per_device(): lax.all_to_all(sent_bins, 'dp', split_axis=0, concat_axis=0, tiled=True)  7.36 us
    while x46, local copies, waits for them, and re-layouts  7.26 us
    all_to_all x1, waiting for transfers between devices, per_device(): lax.all_to_all(sent_wave, 'dp', split_axis=0, concat_axis=0, tiled=True)  5.32 us
    dot_general x2, matrix products, pass_group(): jnp.dot(cols_two, conv_two, preferred_element_type=jnp.float32) + bias_two  4.2 us
    dot_general x1, matrix products, per_device(): lax.dot_general(cols_all, dz_all, (((0,), (0,)), ((), ())), preferred_ele...  4.2 us
    all_to_all x1, waiting for transfers between devices, per_device(): lax.all_to_all(sent_bins, 'dp', split_axis=0, concat_axis=0, tiled=True)  3.87 us
  transfers between devices with their start and end apart: 4, of which 3 were waited for; matrix products, arithmetic and copies ran while one was open for 2% of the time, Pallas kernels for 0%

commit v1 on v0

--- a/solution.py
+++ b/solution.py
@@ -2,6 +2,7 @@
 import jax.numpy as jnp
 from jax import lax
 from jax.sharding import PartitionSpec as P
+from jax.lax import psum
 
 NB = 4
 GROUP = 8
@@ -153,7 +154,8 @@
     )
     whole = lax.psum(term, "blk")
     share = lax.psum_scatter(whole, "dp", scatter_dimension=0, tiled=True)
-    small_total = lax.psum(small_local, ("dp", "blk"))
+    all_rows = psum(small_local, "blk")
+    small_total = psum(all_rows, axis_name="dp")
     return (share, small_total)
 
 

time: 193 us -> 220 us (1.14)
  blocking collectives: 40.6 us -> 67.2 us
    psum x1 -> x2, blocking collectives: 40.6 us -> 67.2 us  [the longest x1 58.2 us: per_device(): small_total = psum(all_rows, axis_name='dp')]
where the time goes in v1:
time: 220 us; the launch traced here: 219 us
  waiting for transfers between devices  72.8 us (33%)
  blocking collectives  67.2 us (31%)
  local copies, waits for them, and re-layouts  25.6 us (12%)
  other arithmetic  16.9 us (8%)
  between operations  14.1 us (6%)
  starting transfers between devices  10.9 us (5%)
  matrix products  10.8 us (5%)
    reduce_scatter x1, waiting for transfers between devices, per_device(): share = lax.psum_scatter(whole, 'dp', scatter_dimension=0, tiled=True)  63.6 us
    psum x1, blocking collectives, per_device(): small_total = psum(all_rows, axis_name='dp')  58.2 us
    psum x1, blocking collectives, per_device(): all_rows = psum(small_local, 'blk')  9.02 us
    all_to_all x1, starting transfers between devices, per_device(): lax.all_to_all(sent_bins, 'dp', split_axis=0, concat_axis=0, tiled=True)  7.36 us
    while x46, local copies, waits for them, and re-layouts  7.26 us
    all_to_all x1, waiting for transfers between devices, per_device(): lax.all_to_all(sent_wave, 'dp', split_axis=0, concat_axis=0, tiled=True)  5.32 us
  transfers between devices with their start and end apart: 4, of which 3 were waited for; matrix products, arithmetic and copies ran while one was open for 2% of the time, Pallas kernels for 0%

profile of v1, /device:TPU:0, one launch (start us, length us, event | category | flops | bytes accessed | tf_op | source)
XLA Modules:
  0.0 219.0 jit_solution(13434741510211362902)
XLA Ops:
  7.2 0.7 fusion.21
  7.9 1.3 gather_fusion.1
  9.2 0.7 copy.29
  9.9 7.4 %all-to-all-start.1 = ((s32[16,1,1]{2,1,0:T(1,128)}), s32[16,1,1]{2,1,0:T(1,128)S(1)}, u32[]{:S(2)}, u32[]{:S(2)}) async-start(s32[16,1,1]{2,1,0:T(1,128)} %copy.29), calls=%async_computation.1 | async-start | bytes 16384 | tf_op jit(solution)/shard_map/all_to_all | solution.py:120
  17.2 0.6 gather_fusion
  17.8 0.5 broadcast.360
  18.3 0.7 reduce.1
  19.0 0.7 reshape.260
  19.7 3.9 %all-to-all-done.1 = s32[16,1,1]{2,1,0:T(1,128)S(1)} async-done(((s32[16,1,1]{2,1,0:T(1,128)}), s32[16,1,1]{2,1,0:T(1,128)S(1)}, u32[]{:S(2)}, u32[]{:S(2)}) %all-to-all-start.1) | async-done | bytes 96 | tf_op jit(solution)/shard_map/all_to_all | solution.py:120
  23.6 3.5 %all-to-all-start = ((bf16[16,2,165]{2,1,0:T(2,128)(2,1)}), bf16[16,2,165]{2,1,0:T(2,128)(2,1)S(1)}, u32[]{:S(2)}, u32[]{:S(2)}) async-start(bf16[16,2,165]{2,1,0:T(2,128)(2,1)} %reshape.260), calls=%async_computation | async-start | bytes 32768 | tf_op jit(solution)/shard_map/all_to_all | solution.py:119
  27.5 0.7 reshape.230
  28.2 5.3 %all-to-all-done = bf16[16,2,165]{2,1,0:T(2,128)(2,1)S(1)} async-done(((bf16[16,2,165]{2,1,0:T(2,128)(2,1)}), bf16[16,2,165]{2,1,0:T(2,128)(2,1)S(1)}, u32[]{:S(2)}, u32[]{:S(2)}) %all-to-all-start) | async-done | bytes 10592 | tf_op jit(solution)/shard_map/all_to_all | solution.py:119
  33.6 0.6 copy.35
  34.2 41.1 %while.17 = (s32[]{:T(128)}, f32[16,512]{1,0:T(8,128)}, bf16[2,256,1536]{2,1,0:T(8,128)(2,1)}, bf16[2,256,512]{2,1,0:T(8,128)(2,1)}, bf16[2,8,330]{2,1,0:T(8,128...) while((s32[]{:T(128)}, f32[16,512]{1,0:T(8,128)}, ...), condition=%wide.region_15.16_spmd.clone, body=%wide.region_0.15_spmd.clone.sunk | while | flops 835685888 | bytes 56027588 | solution.py:149
  34.2 0.7 and_select_fusion.2
  35.1 0.7 constant_dynamic-slice_fusion.5
  36.6 0.4 fusion.58
  39.0 2.1 fusion.59
  41.4 0.6 multiply_reduce_fusion.14
  42.4 0.8 copy-done.10
  43.3 0.9 maximum_dynamic-update-slice_fusion.2
  44.2 0.8 copy-done.1
  45.0 0.6 fusion.61
  45.6 0.8 slice_bitcast_fusion.2
  46.7 1.6 copy.42
  48.6 1.7 reshape.273
  50.4 1.5 pad_add_fusion.2
  52.0 1.1 multiply_reduce_fusion.15
  53.8 0.6 select_add_fusion.2
  54.4 0.7 and_select_fusion.2
  55.3 0.7 constant_dynamic-slice_fusion.5
  59.2 2.1 fusion.59
  61.6 0.6 multiply_reduce_fusion.14
  62.6 0.8 copy-done.10
  63.5 0.9 maximum_dynamic-update-slice_fusion.2
  64.4 0.8 copy-done.1
  65.2 0.6 fusion.61
  65.8 0.8 slice_bitcast_fusion.2
  66.9 1.6 copy.42
  68.8 1.7 reshape.273
  70.6 1.5 pad_add_fusion.2
  72.2 1.1 multiply_reduce_fusion.15
  74.0 1.4 select_add_fusion.2
  75.4 4.2 %convolution_bitcast_fusion = f32[1536,512]{1,0:T(8,128)} fusion(bf16[2,256,1536]{2,1,0:T(8,128)(2,1)} %get-tuple-element.190, bf16[2,256,512]{2,1,0:T(8,128)(2,1)} %get-tuple-element.191), kind=kOutput, calls=%fused_computation.65 | convolution fusion | flops 805306368 | bytes 5242880 | tf_op jit(solution)/shard_map/dot_general | solution.py:152
  79.6 63.6 %reduce-scatter.2.cloned.1.call-done = f32[96,512]{1,0:T(8,128)} async-done(((f32[1536,512]{1,0:T(8,128)}), f32[96,512]{1,0:T(8,128)}) %reduce-scatter.2.cloned.1.call-update) | async-done | bytes 196624 | tf_op jit(solution)/shard_map/reduce_scatter | solution.py:156
  143.3 9.0 %psum.22 = f32[16,512]{1,0:T(8,128)S(1)} all-reduce(f32[16,512]{1,0:T(8,128)} %get-tuple-element.192), channel_id=1, replica_groups=mesh['dp'=16,'blk'=2] {'blk'}, use_global_device_ids=true, to_apply=%region_18.19 | all-reduce | flops 8192 | bytes 65536 | tf_op jit(solution)/shard_map/psum | solution.py:157
  152.3 58.2 %psum.23 = f32[16,512]{1,0:T(8,128)} all-reduce(f32[16,512]{1,0:T(8,128)S(1)} %psum.22), channel_id=1, replica_groups=mesh['dp'=16,'blk'=2] {'dp'}, use_global_device_ids=true, to_apply=%region_19.20 | all-reduce | flops 8192 | bytes 65536 | tf_op jit(solution)/shard_map/psum | solution.py:158
  210.5 1.6 copy.58
  (120 shorter events, 10.7 us)
Async XLA Ops:
  7.2 10.1 %copy-start = (bf16[16,330]{1,0:T(8,128)(2,1)S(1)}, bf16[16,330]{1,0:T(8,128)(2,1)}, u32[]{:S(2)}) copy-start(bf16[16,330]{1,0:T(8,128)(2,1)} %param.14) | copy-start | bytes 31684
  9.9 13.7 %all-to-all-start.1 = ((s32[16,1,1]{2,1,0:T(1,128)}), s32[16,1,1]{2,1,0:T(1,128)S(1)}, u32[]{:S(2)}, u32[]{:S(2)}) async-start(s32[16,1,1]{2,1,0:T(1,128)} %copy.29), calls=%async_computation.1 | async-start | bytes 16384 | tf_op jit(solution)/shard_map/all_to_all | solution.py:120
  23.6 10.0 %all-to-all-start = ((bf16[16,2,165]{2,1,0:T(2,128)(2,1)}), bf16[16,2,165]{2,1,0:T(2,128)(2,1)S(1)}, u32[]{:S(2)}, u32[]{:S(2)}) async-start(bf16[16,2,165]{2,1,0:T(2,128)(2,1)} %reshape.260), calls=%async_computation | async-start | bytes 32768 | tf_op jit(solution)/shard_map/all_to_all | solution.py:119
  27.1 116.2 %reduce-scatter.2.cloned.1.call-start = ((), (), s32[]{:S(2)}) async-start(), calls=%async_computation.3 | async-start | bytes 3342336 | tf_op jit(solution)/shard_map/reduce_scatter | solution.py:156
  34.2 2.3 %copy-start.2 = (bf16[2,8,32,512]{3,2,1,0:T(8,128)(2,1)S(1)}, bf16[2,8,32,512]{3,2,1,0:T(8,128)(2,1)}, u32[]{:S(2)}) copy-start(bf16[2,8,32,512]{3,2,1,0:T(8,128)(2,1)} %get-tuple-element.477) | copy-start | bytes 1572868 | tf_op jit(solution)/shard_map/while
  34.2 2.3 %copy-start.4 = (bf16[10,512]{1,0:T(8,128)(2,1)S(1)}, bf16[10,512]{1,0:T(8,128)(2,1)}, u32[]{:S(2)}) copy-start(bf16[10,512]{1,0:T(8,128)(2,1)} %get-tuple-element.471) | copy-start | bytes 30724 | tf_op jit(solution)/shard_map/while
  34.2 2.3 %copy-start.7 = (f32[512]{0:T(512)S(1)}, f32[512]{0:T(512)}, u32[]{:S(2)}) copy-start(f32[512]{0:T(512)} %get-tuple-element.472) | copy-start | bytes 6148 | tf_op jit(solution)/shard_map/while
  36.5 0.8 copy-start.3
  36.5 0.8 copy-start.5
  38.4 0.7 copy-start.11
  39.0 2.3 %copy-start.6 = (f32[512]{0:T(512)S(1)}, f32[512]{0:T(512)}, u32[]{:S(2)}) copy-start(f32[512]{0:T(512)} %get-tuple-element.479) | copy-start | bytes 6148 | tf_op jit(solution)/shard_map/while
  39.0 2.3 %copy-start.8 = (f32[512]{0:T(512)S(1)}, f32[512]{0:T(512)}, u32[]{:S(2)}) copy-start(f32[512]{0:T(512)} %get-tuple-element.480) | copy-start | bytes 6148 | tf_op jit(solution)/shard_map/while
  41.1 1.0 copy-start.9
  42.4 0.8 copy-start.10
  43.3 1.7 copy-start.1
  54.4 2.3 %copy-start.2 = (bf16[2,8,32,512]{3,2,1,0:T(8,128)(2,1)S(1)}, bf16[2,8,32,512]{3,2,1,0:T(8,128)(2,1)}, u32[]{:S(2)}) copy-start(bf16[2,8,32,512]{3,2,1,0:T(8,128)(2,1)} %get-tuple-element.477) | copy-start | bytes 1572868 | tf_op jit(solution)/shard_map/while
  54.4 2.3 %copy-start.4 = (bf16[10,512]{1,0:T(8,128)(2,1)S(1)}, bf16[10,512]{1,0:T(8,128)(2,1)}, u32[]{:S(2)}) copy-start(bf16[10,512]{1,0:T(8,128)(2,1)} %get-tuple-element.471) | copy-start | bytes 30724 | tf_op jit(solution)/shard_map/while
  54.4 2.3 %copy-start.7 = (f32[512]{0:T(512)S(1)}, f32[512]{0:T(512)}, u32[]{:S(2)}) copy-start(f32[512]{0:T(512)} %get-tuple-element.472) | copy-start | bytes 6148 | tf_op jit(solution)/shard_map/while
  56.7 0.8 copy-start.3
  56.7 0.8 copy-start.5
  58.6 0.7 copy-start.11
  59.2 2.3 %copy-start.6 = (f32[512]{0:T(512)S(1)}, f32[512]{0:T(512)}, u32[]{:S(2)}) copy-start(f32[512]{0:T(512)} %get-tuple-element.479) | copy-start | bytes 6148 | tf_op jit(solution)/shard_map/while
  59.2 2.3 %copy-start.8 = (f32[512]{0:T(512)S(1)}, f32[512]{0:T(512)}, u32[]{:S(2)}) copy-start(f32[512]{0:T(512)} %get-tuple-element.480) | copy-start | bytes 6148 | tf_op jit(solution)/shard_map/while
  61.3 1.0 copy-start.9
  62.6 0.8 copy-start.10
  63.5 1.7 copy-start.1
  79.6 130.9 %all-reduce.5.cloned.1.call-start = ((), (), s32[]{:S(2)}) async-start(), calls=%async_computation.4 | async-start | bytes 393216 | tf_op jit(solution)/shard_map/psum | solution.py:155
Sparse Core Ops, SparseCore 0:
  79.7 63.4 reduce-scatter.1
  145.5 21.3 all-reduce.4
